TPU v7x, 32 devices: a whole 2x2x4 slice. The times are simulated.
32 devices in a mesh: dp: 8 (over z, x), seq: 4 (over y, core).
Axes of the slice: x: 2, y: 2, z: 4, core: 2. Of those that a mesh axis runs over, the one named last changes fastest.
Arguments:
- tokens: bfloat16 [8192, 512], P(('dp', 'seq')), may hold values from -6 to 6
- memory: bfloat16 [8192, 512], P(('dp', 'seq')), may hold values from -6 to 6
- cotangent: bfloat16 [8192, 512], P(('dp', 'seq')), may hold values from -6 to 6
- arrival_order: int32 [8192], replicated, may hold values from 0 to 8191, as said below
- lengths: int32 [64], replicated, may hold values from 1 to 512, as said below
- real_flag: int32 [64], replicated, may hold values from 0 to 1, as said below
- self_proj: bfloat16 [3, 512, 512], replicated, may hold values from -0.25 to 0.25
- cross_proj: bfloat16 [3, 512, 512], replicated, may hold values from -0.25 to 0.25
- mixers: bfloat16 [2, 512, 512], replicated, may hold values from -1 to 1
- expander: bfloat16 [512, 2048], replicated, may hold values from -0.25 to 0.25
- shrinker: bfloat16 [2048, 512], replicated, may hold values from -0.125 to 0.125
- norm_gains: float32 [3, 512], replicated, may hold values from 0.5 to 1.5
- norm_shifts: float32 [3, 512], replicated, may hold values from -0.5 to 0.5
Outputs:
- layer_out: bfloat16 [8192, 512], P(('dp', 'seq'))
- token_grad: bfloat16 [8192, 512], P(('dp', 'seq'))
- memory_grad: bfloat16 [8192, 512], P(('dp', 'seq'))
- self_grad: float32 [3, 512, 512], replicated
- cross_grad: float32 [3, 512, 512], replicated
- mixers_grad: float32 [2, 512, 512], replicated
- expander_grad: float32 [512, 2048], replicated
- shrinker_grad: float32 [2048, 512], replicated
- gains_grad: float32 [3, 512], replicated
- shifts_grad: float32 [3, 512], replicated
Inputs may be any that keep to these rules, and one draw needn't show every extreme that they name: `arrival_order`: A permutation. Sentences stand in id order, token t of sentence j being position t - (sum of the lengths of sentences before j). The rows of one device hold tokens of sentences of exactly 4 bucket groups, 64 rows for each of them; the devices with one seq index together hold exactly 256 tokens of each bucket group. `lengths`: bucket group g holds the 8 sentences g * 8 to (g + 1) * 8 - 1; they have 4 * 256 tokens together, and one of them has 512. `real_flag`: A group's sentence of 512 tokens is real.
All inputs are finite; a program needn't handle non-finite values.
Results may differ from a plain program's by a relative error of at most 0.025.
Values may be sent and summed in bfloat16 or wider, within the bound.
A program may use at most 128 MiB of HBM per device.

v0:
```python
import jax
import jax.numpy as jnp
from jax import lax
from jax.sharding import PartitionSpec as P

HEAD = 64


synth_weight = 0.4
score_fill = -1e30
epsilon = 1e-05


def normalize(values, gain, shift):
    center = values - jnp.mean(values, axis=-1, keepdims=True)
    spread = jnp.mean(center * center, axis=-1, keepdims=True)
    return center * lax.rsqrt(spread + epsilon) * gain + shift


def split_pairs(matrix):
    return matrix.reshape(matrix.shape[0], -1, 2 * HEAD).transpose(1, 0, 2)


def join_pairs(stacked):
    return stacked.transpose(1, 0, 2).reshape(stacked.shape[1], -1)


def as_heads(matrix):
    return matrix.reshape(matrix.shape[0], 2, HEAD)


def pair_scores(query_pair, key_pair, allowed):
    scores = jnp.einsum(
        "qhd,khd->hqk", as_heads(query_pair), as_heads(key_pair), preferred_element_type=jnp.float32
    ) * HEAD ** (-0.5)
    return jnp.where(allowed[None], scores, score_fill)


def attend_forward(queries, keys_all, values_all, allowed):

    def one_pair(items):
        query_pair, key_pair, value_pair = items
        scores = pair_scores(query_pair, key_pair, allowed)
        peak = jnp.max(scores, axis=-1, keepdims=True)
        lifted = jnp.exp(scores - peak)
        total = jnp.sum(lifted, axis=-1, keepdims=True)
        probs = (lifted / total).astype(jnp.bfloat16)
        mixed = jnp.einsum(
            "hqk,khd->qhd", probs, as_heads(value_pair), preferred_element_type=jnp.float32
        )
        return (mixed.reshape(query_pair.shape[0], -1), (peak + jnp.log(total))[..., 0])

    mixed, logsum = lax.map(
        one_pair, (split_pairs(queries), split_pairs(keys_all), split_pairs(values_all))
    )
    return (join_pairs(mixed), logsum)


def attend_backward(queries, keys_all, values_all, allowed, logsum, mixed_grad):

    def one_pair(items):
        query_pair, key_pair, value_pair, pair_logsum, grad_pair, pair_inner = items
        scores = pair_scores(query_pair, key_pair, allowed)
        probs = jnp.exp(scores - pair_logsum[..., None])
        probs_low = probs.astype(jnp.bfloat16)
        grad_heads = as_heads(grad_pair)
        value_grad = jnp.einsum(
            "hqk,qhd->khd", probs_low, grad_heads, preferred_element_type=jnp.float32
        )
        prob_grad = jnp.einsum(
            "qhd,khd->hqk", grad_heads, as_heads(value_pair), preferred_element_type=jnp.float32
        )
        inner = jnp.sum(probs * prob_grad, axis=-1, keepdims=True)
        score_grad = (probs * (prob_grad - inner)).astype(jnp.bfloat16)
        query_grad = jnp.einsum(
            "hqk,khd->qhd", score_grad, as_heads(key_pair), preferred_element_type=jnp.float32
        ) * HEAD ** (-0.5)
        key_grad = jnp.einsum(
            "hqk,qhd->khd", score_grad, as_heads(query_pair), preferred_element_type=jnp.float32
        ) * HEAD ** (-0.5)
        width = 2 * HEAD
        return (
            query_grad.reshape(-1, width),
            key_grad.reshape(-1, width),
            value_grad.reshape(-1, width),
            inner[..., 0],
        )

    query_grad, key_grad, value_grad, inner_out = lax.map(
        one_pair,
        (
            split_pairs(queries),
            split_pairs(keys_all),
            split_pairs(values_all),
            logsum,
            split_pairs(mixed_grad),
            logsum,
        ),
    )
    return (join_pairs(query_grad), join_pairs(key_grad), join_pairs(value_grad), inner_out)


def body(
    tokens,
    memory,
    cotangent,
    arrival_order,
    lengths,
    real_flag,
    self_proj,
    cross_proj,
    mixers,
    expander,
    shrinker,
    norm_gains,
    norm_shifts,
):
    n_groups = lax.axis_size("dp")
    n_lanes = lax.axis_size("seq")
    rows = tokens.shape[0]
    width = tokens.shape[1]
    capacity = 2 * rows // n_groups
    slots = n_groups * capacity
    n_half = n_groups // 2
    group = lax.axis_index("dp")
    lane = lax.axis_index("seq")
    ends = jnp.cumsum(lengths)
    starts = ends - lengths
    table = arrival_order.reshape(n_groups, n_lanes, rows)
    sentence = jnp.searchsorted(ends, table, side="right")
    position = table - starts[sentence]
    target = starts[sentence] // (n_lanes * rows)
    onehot = target[..., None] == jnp.arange(n_groups, dtype=jnp.int32)
    ranks = jnp.cumsum(onehot.astype(jnp.int32), axis=2)
    slot = jnp.sum(jnp.where(onehot, ranks, 0), axis=-1) - 1
    row_weight = jnp.where(real_flag[sentence] > 0, 1.0, synth_weight).astype(jnp.float32)
    place = target[group, lane] * capacity + slot[group, lane]
    source = jnp.zeros((slots,), jnp.int32).at[place].set(jnp.arange(rows, dtype=jnp.int32))
    filled = jnp.zeros((slots,), jnp.bool_).at[place].set(True)

    def packed(values):
        picked = jnp.where(filled[:, None], values[source], jnp.zeros((), values.dtype))
        return picked.reshape(n_groups, capacity, width)

    arrived_tokens, arrived_memory, arrived_cot = (
        lax.all_to_all(packed(tokens), "dp", split_axis=0, concat_axis=0, tiled=True),
        lax.all_to_all(packed(memory), "dp", split_axis=0, concat_axis=0, tiled=True),
        lax.all_to_all(packed(cotangent), "dp", split_axis=0, concat_axis=0, tiled=True),
    )
    senders = jnp.any(target == group, axis=2).T.astype(jnp.int32)
    sender_rank = jnp.cumsum(senders, axis=1) - 1
    lane_rows = jnp.broadcast_to(jnp.arange(n_lanes, dtype=jnp.int32)[:, None], (n_lanes, n_groups))
    picked_sources = (
        jnp.zeros((n_lanes, n_half), jnp.int32)
        .at[lane_rows, jnp.where(senders > 0, sender_rank, n_half)]
        .set(
            jnp.broadcast_to(jnp.arange(n_groups, dtype=jnp.int32)[None, :], (n_lanes, n_groups)),
            mode="drop",
        )
    )
    compact_slot = (
        picked_sources[:, :, None] * capacity + jnp.arange(capacity, dtype=jnp.int32)[None, None, :]
    ).reshape(n_lanes, rows)
    my_slot = lax.dynamic_index_in_dim(compact_slot, lane, 0, keepdims=False)
    arrived_tokens = arrived_tokens.reshape(slots, width)[my_slot]
    arrived_memory = arrived_memory.reshape(slots, width)[my_slot]
    arrived_cot = arrived_cot.reshape(slots, width)[my_slot]
    source_slot = jnp.arange(n_groups, dtype=jnp.int32)[:, None, None] * capacity + slot
    landing = jnp.where(
        target == group,
        jnp.arange(n_lanes, dtype=jnp.int32)[None, :, None] * slots + source_slot,
        n_lanes * slots,
    ).ravel()
    slot_sentence = (
        jnp.full((n_lanes * slots,), -1, jnp.int32)
        .at[landing]
        .set(sentence.ravel(), mode="drop")
        .reshape(n_lanes, slots)
    )
    slot_position = (
        jnp.zeros((n_lanes * slots,), jnp.int32)
        .at[landing]
        .set(position.ravel(), mode="drop")
        .reshape(n_lanes, slots)
    )
    slot_weight = (
        jnp.zeros((n_lanes * slots,), jnp.float32)
        .at[landing]
        .set(row_weight.ravel(), mode="drop")
        .reshape(n_lanes, slots)
    )
    lane_sentence = jnp.take_along_axis(slot_sentence, compact_slot, axis=1)
    lane_position = jnp.take_along_axis(slot_position, compact_slot, axis=1)
    lane_weight = jnp.take_along_axis(slot_weight, compact_slot, axis=1)
    key_sentence = lane_sentence.reshape(-1)
    key_position = lane_position.reshape(-1)
    query_sentence = lax.dynamic_index_in_dim(lane_sentence, lane, 0, keepdims=False)
    query_position = lax.dynamic_index_in_dim(lane_position, lane, 0, keepdims=False)
    query_weight = lax.dynamic_index_in_dim(lane_weight, lane, 0, keepdims=False)
    same_sentence = key_sentence[None, :] == query_sentence[:, None]
    self_allowed = same_sentence & (key_position[None, :] <= query_position[:, None])
    self_qkv = jnp.einsum(
        "rd,jde->jre", arrived_tokens, self_proj, preferred_element_type=jnp.float32
    ).astype(jnp.bfloat16)
    keys_all, values_all = (
        lax.all_gather(self_qkv[1], "seq", axis=0, tiled=True),
        lax.all_gather(self_qkv[2], "seq", axis=0, tiled=True),
    )
    self_mixed, self_logsum = attend_forward(self_qkv[0], keys_all, values_all, self_allowed)
    self_mixed_low = self_mixed.astype(jnp.bfloat16)
    first_sum = arrived_tokens.astype(jnp.float32) + jnp.dot(
        self_mixed_low, mixers[0], preferred_element_type=jnp.float32
    )
    first_norm, first_back = jax.vjp(normalize, first_sum, norm_gains[0], norm_shifts[0])
    first_low = first_norm.astype(jnp.bfloat16)
    cross_queries = jnp.dot(first_low, cross_proj[0], preferred_element_type=jnp.float32).astype(
        jnp.bfloat16
    )
    memory_kv = jnp.einsum(
        "rd,jde->jre", arrived_memory, cross_proj[1:], preferred_element_type=jnp.float32
    ).astype(jnp.bfloat16)
    memory_keys, memory_values = (
        lax.all_gather(memory_kv[0], "seq", axis=0, tiled=True),
        lax.all_gather(memory_kv[1], "seq", axis=0, tiled=True),
    )
    cross_mixed, cross_logsum = attend_forward(
        cross_queries, memory_keys, memory_values, same_sentence
    )
    cross_mixed_low = cross_mixed.astype(jnp.bfloat16)
    second_sum = first_norm + jnp.dot(
        cross_mixed_low, mixers[1], preferred_element_type=jnp.float32
    )
    second_norm, second_back = jax.vjp(normalize, second_sum, norm_gains[1], norm_shifts[1])
    second_low = second_norm.astype(jnp.bfloat16)
    hidden_pre = jnp.dot(second_low, expander, preferred_element_type=jnp.float32)
    hidden_act, silu_back = jax.vjp(jax.nn.silu, hidden_pre)
    hidden_low = hidden_act.astype(jnp.bfloat16)
    third_sum = second_norm + jnp.dot(hidden_low, shrinker, preferred_element_type=jnp.float32)
    result, third_back = jax.vjp(normalize, third_sum, norm_gains[2], norm_shifts[2])
    result_low = result.astype(jnp.bfloat16)
    weighted_cot = arrived_cot.astype(jnp.float32) * query_weight[:, None]
    third_grad, gain_three, shift_three = third_back(weighted_cot)
    branch_three = third_grad.astype(jnp.bfloat16)
    shrinker_grad = jnp.einsum(
        "rf,rd->fd", hidden_low, branch_three, preferred_element_type=jnp.float32
    )
    hidden_grad = jnp.einsum(
        "rd,fd->rf", branch_three, shrinker, preferred_element_type=jnp.float32
    )
    pre_grad = silu_back(hidden_grad)[0].astype(jnp.bfloat16)
    expander_grad = jnp.einsum(
        "rd,rf->df", second_low, pre_grad, preferred_element_type=jnp.float32
    )
    second_total = third_grad + jnp.einsum(
        "rf,df->rd", pre_grad, expander, preferred_element_type=jnp.float32
    )
    second_grad, gain_two, shift_two = second_back(second_total)
    branch_two = second_grad.astype(jnp.bfloat16)
    mixer_cross = jnp.einsum(
        "rd,re->de", cross_mixed_low, branch_two, preferred_element_type=jnp.float32
    )
    cross_mixed_grad = jnp.einsum(
        "re,de->rd", branch_two, mixers[1], preferred_element_type=jnp.float32
    ).astype(jnp.bfloat16)
    cross_query_grad, memory_key_part, memory_value_part, cross_inner = attend_backward(
        cross_queries, memory_keys, memory_values, same_sentence, cross_logsum, cross_mixed_grad
    )
    memory_key_grad, memory_value_grad = (
        lax.psum_scatter(
            memory_key_part.astype(jnp.bfloat16), "seq", scatter_dimension=0, tiled=True
        ).astype(jnp.float32),
        lax.psum_scatter(
            memory_value_part.astype(jnp.bfloat16), "seq", scatter_dimension=0, tiled=True
        ).astype(jnp.float32),
    )
    memory_kv_grad = jnp.stack([memory_key_grad, memory_value_grad]).astype(jnp.bfloat16)
    cross_query_low = cross_query_grad.astype(jnp.bfloat16)
    cross_grad = jnp.concatenate(
        [
            jnp.einsum("rd,re->de", first_low, cross_query_low, preferred_element_type=jnp.float32)[
                None
            ],
            jnp.einsum(
                "rd,jre->jde", arrived_memory, memory_kv_grad, preferred_element_type=jnp.float32
            ),
        ],
        axis=0,
    )
    memory_in_grad = jnp.einsum(
        "jre,jde->rd", memory_kv_grad, cross_proj[1:], preferred_element_type=jnp.float32
    ).astype(jnp.bfloat16)
    first_total = second_grad + jnp.einsum(
        "re,de->rd", cross_query_low, cross_proj[0], preferred_element_type=jnp.float32
    )
    first_grad, gain_one, shift_one = first_back(first_total)
    branch_one = first_grad.astype(jnp.bfloat16)
    mixer_self = jnp.einsum(
        "rd,re->de", self_mixed_low, branch_one, preferred_element_type=jnp.float32
    )
    self_mixed_grad = jnp.einsum(
        "re,de->rd", branch_one, mixers[0], preferred_element_type=jnp.float32
    ).astype(jnp.bfloat16)
    self_query_grad, key_part, value_part, self_inner = attend_backward(
        self_qkv[0], keys_all, values_all, self_allowed, self_logsum, self_mixed_grad
    )
    key_grad, value_grad = (
        lax.psum_scatter(
            key_part.astype(jnp.bfloat16), "seq", scatter_dimension=0, tiled=True
        ).astype(jnp.float32),
        lax.psum_scatter(
            value_part.astype(jnp.bfloat16), "seq", scatter_dimension=0, tiled=True
        ).astype(jnp.float32),
    )
    self_qkv_grad = jnp.stack([self_query_grad, key_grad, value_grad]).astype(jnp.bfloat16)
    self_grad = jnp.einsum(
        "rd,jre->jde", arrived_tokens, self_qkv_grad, preferred_element_type=jnp.float32
    )
    token_in_grad = (
        first_grad
        + jnp.einsum("jre,jde->rd", self_qkv_grad, self_proj, preferred_element_type=jnp.float32)
    ).astype(jnp.bfloat16)
    all_sums = lax.psum(
        (
            self_grad,
            cross_grad,
            jnp.stack([mixer_self, mixer_cross]),
            expander_grad,
            shrinker_grad,
            jnp.stack([gain_one, gain_two, gain_three]),
            jnp.stack([shift_one, shift_two, shift_three]),
        ),
        ("dp", "seq"),
    )
    self_total = all_sums[0]
    cross_total = all_sums[1]
    mixers_total = all_sums[2]
    expander_total = all_sums[3]
    shrinker_total = all_sums[4]
    gains_total = all_sums[5]
    shifts_total = all_sums[6]

    def spread_out(values):
        return (
            jnp.zeros((slots, width), values.dtype)
            .at[my_slot]
            .set(values)
            .reshape(n_groups, capacity, width)
        )

    back_out, back_tokens, back_memory = (
        lax.all_to_all(spread_out(result_low), "dp", split_axis=0, concat_axis=0, tiled=True),
        lax.all_to_all(spread_out(token_in_grad), "dp", split_axis=0, concat_axis=0, tiled=True),
        lax.all_to_all(spread_out(memory_in_grad), "dp", split_axis=0, concat_axis=0, tiled=True),
    )
    layer_out = back_out.reshape(slots, width)[place]
    token_grad = back_tokens.reshape(slots, width)[place]
    memory_grad = back_memory.reshape(slots, width)[place]
    return (
        layer_out,
        token_grad,
        memory_grad,
        self_total,
        cross_total,
        mixers_total,
        expander_total,
        shrinker_total,
        gains_total,
        shifts_total,
    )


def solution(mesh):
    placed = (
        P(("dp", "seq"), None),
        P(("dp", "seq"), None),
        P(("dp", "seq"), None),
        P(),
        P(),
        P(),
        P(),
        P(),
        P(),
        P(),
        P(),
        P(),
        P(),
    )
    return jax.shard_map(
        body,
        mesh=mesh,
        in_specs=placed,
        out_specs=(
            P(("dp", "seq"), None),
            P(("dp", "seq"), None),
            P(("dp", "seq"), None),
            P(),
            P(),
            P(),
            P(),
            P(),
            P(),
            P(),
        ),
        check_vma=False,
    )
```

profile of v0, /device:TPU:0, one launch (start us, length us, event | category | flops | bytes accessed | tf_op | source)
XLA Modules:
  0.0 1498.4 jit_solution(13586645068352639001)
XLA Ops:
  9.8 343.5 %while.90 = (s32[]{:T(128)}, u32[8,4,256]{2,1,0:T(4,128)S(1)}, u32[8,4,256]{2,1,0:T(4,128)S(1)}, s32[64]{0:T(128)S(1)}, s32[8,4,256]{2,1,0:T(4,128)S(1)}, /*index=5*/s32[]{:T(128)}, s32[]{:T(128)}, s32[]{}) while((s32[]{:T(128)}, u32[8,4,256]{2,1,0:T(4,128)S(1)}, u32[8,4,256]{2,1,0:T(4,128)S(1)}, s32[64]{0:T(128)S(1)}, ...), condition=%wide.region_2.3_spmd.clone, body=%wide.region_1.2_spmd.clone.sunk | while | flops 155652 | bytes 737397 | solution.py:130
  9.9 48.9 %gather_fusion = s32[8192]{0:T(1024)S(1)} fusion(s32[64]{0:T(128)S(1)} %get-tuple-element.932, u32[8192]{0:T(1024)S(1)} %broadcast_clamp_fusion.3), kind=kCustom, calls=%fused_computation.clone.clone.1 | custom fusion | bytes 98304 | tf_op jit(solution)/shard_map/jit(searchsorted)/jit(_searchsorted_scan_impl)/vmap(jit(_searchsorted_scan_impl))/while/body/eval_jaxpr/gather | solution.py:130
  58.9 48.9 %gather_fusion = s32[8192]{0:T(1024)S(1)} fusion(s32[64]{0:T(128)S(1)} %get-tuple-element.932, u32[8192]{0:T(1024)S(1)} %broadcast_clamp_fusion.3), kind=kCustom, calls=%fused_computation.clone.clone.1 | custom fusion | bytes 98304 | tf_op jit(solution)/shard_map/jit(searchsorted)/jit(_searchsorted_scan_impl)/vmap(jit(_searchsorted_scan_impl))/while/body/eval_jaxpr/gather | solution.py:130
  108.0 48.9 %gather_fusion = s32[8192]{0:T(1024)S(1)} fusion(s32[64]{0:T(128)S(1)} %get-tuple-element.932, u32[8192]{0:T(1024)S(1)} %broadcast_clamp_fusion.3), kind=kCustom, calls=%fused_computation.clone.clone.1 | custom fusion | bytes 98304 | tf_op jit(solution)/shard_map/jit(searchsorted)/jit(_searchsorted_scan_impl)/vmap(jit(_searchsorted_scan_impl))/while/body/eval_jaxpr/gather | solution.py:130
  157.1 48.9 %gather_fusion = s32[8192]{0:T(1024)S(1)} fusion(s32[64]{0:T(128)S(1)} %get-tuple-element.932, u32[8192]{0:T(1024)S(1)} %broadcast_clamp_fusion.3), kind=kCustom, calls=%fused_computation.clone.clone.1 | custom fusion | bytes 98304 | tf_op jit(solution)/shard_map/jit(searchsorted)/jit(_searchsorted_scan_impl)/vmap(jit(_searchsorted_scan_impl))/while/body/eval_jaxpr/gather | solution.py:130
  206.1 48.9 %gather_fusion = s32[8192]{0:T(1024)S(1)} fusion(s32[64]{0:T(128)S(1)} %get-tuple-element.932, u32[8192]{0:T(1024)S(1)} %broadcast_clamp_fusion.3), kind=kCustom, calls=%fused_computation.clone.clone.1 | custom fusion | bytes 98304 | tf_op jit(solution)/shard_map/jit(searchsorted)/jit(_searchsorted_scan_impl)/vmap(jit(_searchsorted_scan_impl))/while/body/eval_jaxpr/gather | solution.py:130
  255.2 48.9 %gather_fusion = s32[8192]{0:T(1024)S(1)} fusion(s32[64]{0:T(128)S(1)} %get-tuple-element.932, u32[8192]{0:T(1024)S(1)} %broadcast_clamp_fusion.3), kind=kCustom, calls=%fused_computation.clone.clone.1 | custom fusion | bytes 98304 | tf_op jit(solution)/shard_map/jit(searchsorted)/jit(_searchsorted_scan_impl)/vmap(jit(_searchsorted_scan_impl))/while/body/eval_jaxpr/gather | solution.py:130
  304.3 48.9 %gather_fusion = s32[8192]{0:T(1024)S(1)} fusion(s32[64]{0:T(128)S(1)} %get-tuple-element.932, u32[8192]{0:T(1024)S(1)} %broadcast_clamp_fusion.3), kind=kCustom, calls=%fused_computation.clone.clone.1 | custom fusion | bytes 98304 | tf_op jit(solution)/shard_map/jit(searchsorted)/jit(_searchsorted_scan_impl)/vmap(jit(_searchsorted_scan_impl))/while/body/eval_jaxpr/gather | solution.py:130
  353.4 48.9 %gather_fusion.1 = s32[8192]{0:T(1024)S(1)} fusion(s32[64]{0:T(128)S(1)} %sub.113, s32[8192]{0:T(1024)S(1)} %broadcast_clamp_fusion.1), kind=kCustom, calls=%fused_computation.3 | custom fusion | bytes 98304 | tf_op jit(solution)/shard_map/gather | solution.py:132
  405.2 18.0 %reduce-window.20 = s32[8,4,8,2,128]{4,2,3,1,0:T(8,128)S(1)} reduce-window(s32[8,4,8,2,128]{4,2,3,1,0:T(8,128)S(1)} %fusion.66, s32[]{:T(128)} %copy.178), window={size=1x1x1x1x128 pad=0_0x0_0x0_0x0_0x127_0}, to_apply=%region_6.7 | reduce-window | flops 8323072 | bytes 524292 | tf_op jit(solution)/shard_map/reduce-window.1
  489.7 42.0 %scatter_custom_fusion.4 = s32[2048]{0:T(1024)S(1)} fusion(s32[8192]{0:T(1024)} %bitcast.469, s32[8192]{0:T(1024)S(1)} %sub.119, s32[]{:T(128)} %copy.178), kind=kCustom, calls=%fused_computation.234 | custom fusion | bytes 8704 | tf_op jit(solution)/shard_map/scatter | solution.py:183
  540.9 30.6 %scatter_custom_fusion.3 = s32[2048]{0:T(1024)S(1)} fusion(s32[8192]{0:T(1024)} %bitcast.470, s32[8192]{0:T(1024)S(1)} %bitcast.472, s32[]{:T(128)} %constant.241.clone.1), kind=kCustom, calls=%fused_computation.236 | custom fusion | bytes 8704 | tf_op jit(solution)/shard_map/scatter | solution.py:177
  580.8 48.9 %gather_fusion.9 = s32[8192]{0:T(1024)S(1)} fusion(s32[64]{0:T(128)S(1)} %copy-done.1, s32[8192]{0:T(1024)S(1)} %broadcast_clamp_fusion.1), kind=kCustom, calls=%fused_computation.11 | custom fusion | bytes 98304 | tf_op jit(solution)/shard_map/gather | solution.py:136
  629.7 30.6 %scatter_custom_fusion.6 = f32[2048]{0:T(1024)S(1)} fusion(s32[8192]{0:T(1024)} %bitcast.471, f32[8192]{0:T(1024)S(1)} %compare_select_fusion.6, f32[]{:T(128)} %constant.251.clone.1), kind=kCustom, calls=%fused_computation.232 | custom fusion | bytes 8704 | tf_op jit(solution)/shard_map/scatter | solution.py:189
  676.9 19.4 %while.86 = (s32[]{:T(128)}, bf16[4,256,128]{1,2,0:T(8,128)(2,1)}, f32[4,2,256]{2,1,0:T(2,128)S(1)}, bf16[4,1024,128]{1,2,0:T(8,128)(2,1)S(1)}, bf16[4,256,128]{...) while((s32[]{:T(128)}, bf16[4,256,128]{1,2,0:T(8,128)(2,1)}, ...), condition=%wide.region_16.18_spmd.clone, body=%wide.region_13.17_spmd.clone.sunk | while | flops 141295104 | bytes 9332869 | solution.py:53
  705.9 16.1 %while.87 = (s32[]{:T(128)}, bf16[4,256,128]{1,2,0:T(8,128)(2,1)}, f32[4,2,256]{2,1,0:T(2,128)S(1)}, bf16[4,1024,128]{1,2,0:T(8,128)(2,1)}, bf16[4,256,128]{1,2,...) while((s32[]{:T(128)}, bf16[4,256,128]{1,2,0:T(8,128)(2,1)}, ...), condition=%wide.region_22.24_spmd.clone, body=%wide.region_19.23_spmd.clone.sunk | while | flops 140770816 | bytes 9327733 | solution.py:53
  737.0 33.0 %while.88 = (s32[]{:T(128)}, bf16[4,256,128]{1,2,0:T(8,128)(2,1)}, bf16[4,1024,128]{1,2,0:T(8,128)(2,1)}, bf16[4,1024,128]{1,2,0:T(8,128)(2,1)}, bf16[4,1024,128...) while((s32[]{:T(128)}, bf16[4,256,128]{1,2,0:T(8,128)(2,1)}, ...), condition=%wide.region_35.37_spmd.clone, body=%wide.region_33.36_spmd.clone.sunk | while | flops 340852224 | bytes 20397208 | solution.py:89
  783.6 32.9 %while.89 = (s32[]{:T(128)}, bf16[4,256,128]{1,2,0:T(8,128)(2,1)}, bf16[4,1024,128]{1,2,0:T(8,128)(2,1)}, bf16[4,1024,128]{1,2,0:T(8,128)(2,1)}, bf16[4,1024,128...) while((s32[]{:T(128)}, bf16[4,256,128]{1,2,0:T(8,128)(2,1)}, ...), condition=%wide.region_40.42_spmd.clone, body=%wide.region_38.41_spmd.clone.sunk | while | flops 341376512 | bytes 20402344 | solution.py:89
  838.3 15.4 %reduce-scatter.7.cloned.1.call-done = bf16[256,512]{1,0:T(8,128)(2,1)} async-done(((bf16[1024,512]{1,0:T(8,128)(2,1)}), bf16[256,512]{1,0:T(8,128)(2,1)}) %reduce-scatter.7.cloned.1.call-update) | async-done | bytes 262160 | tf_op jit(solution)/shard_map/reduce_scatter | solution.py:310
  853.7 27.6 %reduce-scatter.5.cloned.1.call-done = bf16[256,512]{1,0:T(8,128)(2,1)} async-done(((bf16[1024,512]{1,0:T(8,128)(2,1)}), bf16[256,512]{1,0:T(8,128)(2,1)}) %reduce-scatter.5.cloned.1.call-update) | async-done | bytes 262160 | tf_op jit(solution)/shard_map/reduce_scatter | solution.py:307
  899.9 14.5 all-to-all-done.2
  922.9 16.2 %all-to-all-done.4 = bf16[8,64,512]{2,1,0:T(8,128)(2,1)S(1)} async-done(((bf16[8,64,512]{2,1,0:T(8,128)(2,1)}), bf16[8,64,512]{2,1,0:T(8,128)(2,1)S(1)}, u32[]{:S(2)}, u32[]{:S(2)}) %all-to-all-start.4) | async-done | bytes 524320 | tf_op jit(solution)/shard_map/all_to_all | solution.py:352
  943.3 40.5 %all-reduce = (f32[3,512]{1,0:T(4,128)}, f32[3,512]{1,0:T(4,128)}) all-reduce(f32[3,512]{1,0:T(4,128)S(1)} %pad_maximum_fusion.8, f32[3,512]{1,0:T(4,128)S(1)} %pad_maximum_fusion.9), channel_id=1, replica_groups=mesh['dp'=8,'seq'=4] {'dp','seq'}, use_global_device_ids=true, to_apply=%region_55.57 | all-reduce | flops 3072 | bytes 24576 | tf_op jit(solution)/shard_map/psum | solution.py:322
  990.6 485.1 %all-reduce.4.cloned.1.call-done = (f32[3,512,512]{1,2,0:T(8,128)}, f32[3,512,512]{1,2,0:T(8,128)}, f32[2,512,512]{2,1,0:T(8,128)}, f32[512,2048]{1,0:T(8,128)}, f32[2048,512]{1,0:T(8,128)}) async-done(((f32[3,512,512]{1,2,0:T(8,128)}, f32[3,512,512]{1,2,0:T(8,128)}, f32[2,512,512]{2,1,0:T(8,128)}, f32[512,2048]{1,0:T(8,128)}, f32[2048,512]{1,0:T(8,128)}), (f32[3,512,512]{1,2,0:T(8,128)}, ...) | async-done | bytes 16777232 | tf_op jit(solution)/shard_map/psum | solution.py:322
  (492 shorter events, 321.4 us)
Async XLA Ops:
  7.2 717.3 %copy-start = (bf16[512,2048]{1,0:T(8,128)(2,1)S(1)}, bf16[512,2048]{1,0:T(8,128)(2,1)}, u32[]{:S(2)}) copy-start(bf16[512,2048]{1,0:T(8,128)(2,1)} %param.34) | copy-start | bytes 6291460
  404.8 22.7 %copy-start.2 = (bf16[256,512]{1,0:T(8,128)(2,1)S(1)}, bf16[256,512]{1,0:T(8,128)(2,1)}, u32[]{:S(2)}) copy-start(bf16[256,512]{1,0:T(8,128)(2,1)} %param.27) | copy-start | bytes 786436
  424.5 20.1 %copy-start.33 = (s32[256,1]{0,1:T(1,128)}, s32[256,1]{0,1:T(1,128)S(1)}, u32[]{:S(2)}) copy-start(s32[256,1]{0,1:T(1,128)S(1)} %get-tuple-element.589) | copy-start | bytes 3076
  437.3 21.7 %all-to-all-start = ((bf16[8,64,512]{2,1,0:T(8,128)(2,1)}), bf16[8,64,512]{2,1,0:T(8,128)(2,1)S(1)}, u32[]{:S(2)}, u32[]{:S(2)}) async-start(bf16[8,64,512]{2,1,0:T(8,128)(2,1)} %get-tuple-element.579), calls=%async_computation | async-start | bytes 1048576 | tf_op jit(solution)/shard_map/all_to_all | solution.py:146
  444.6 227.8 %all-gather.9.cloned.1.call-start = ((), (), s32[]{:S(2)}) async-start(), calls=%async_computation.14 | async-start | bytes 1310720 | tf_op jit(solution)/shard_map/all_gather | solution.py:207
  463.1 18.3 %all-to-all-start.1 = ((bf16[8,64,512]{2,1,0:T(8,128)(2,1)}), bf16[8,64,512]{2,1,0:T(8,128)(2,1)S(1)}, u32[]{:S(2)}, u32[]{:S(2)}) async-start(bf16[8,64,512]{2,1,0:T(8,128)(2,1)} %get-tuple-element.578), calls=%async_computation.1 | async-start | bytes 1048576 | tf_op jit(solution)/shard_map/all_to_all | solution.py:147
  466.8 207.1 %all-gather.11.cloned.1.call-start = ((), (), s32[]{:S(2)}) async-start(), calls=%async_computation.15 | async-start | bytes 1310720 | tf_op jit(solution)/shard_map/all_gather | solution.py:206
  481.4 189.0 %all-to-all-start.3 = ((bf16[8,64,512]{2,1,0:T(8,128)(2,1)}), bf16[8,64,512]{2,1,0:T(8,128)(2,1)S(1)}, u32[]{:S(2)}, u32[]{:S(2)}) async-start(bf16[8,64,512]{2,1,0:T(8,128)(2,1)} %get-tuple-element.577), calls=%async_computation.3 | async-start | bytes 1048576 | tf_op jit(solution)/shard_map/all_to_all | solution.py:148
  485.1 215.5 %all-gather.13.cloned.1.call-start = ((), (), s32[]{:S(2)}) async-start(), calls=%async_computation.16 | async-start | bytes 1310720 | tf_op jit(solution)/shard_map/all_gather | solution.py:224
  489.6 213.3 %all-gather.15.cloned.1.call-start = ((), (), s32[]{:S(2)}) async-start(), calls=%async_computation.17 | async-start | bytes 1310720 | tf_op jit(solution)/shard_map/all_gather | solution.py:223
  660.3 9.2 copy-start.29
  660.3 9.3 copy-start.30
  660.3 9.3 copy-start.25
  672.3 162.3 %reduce-scatter.11.cloned.1.call-start = ((), (), s32[]{:S(2)}) async-start(), calls=%async_computation.13 | async-start | bytes 1310720 | tf_op jit(solution)/shard_map/reduce_scatter | solution.py:272
  772.3 62.3 %reduce-scatter.9.cloned.1.call-start = ((), (), s32[]{:S(2)}) async-start(), calls=%async_computation.12 | async-start | bytes 1310720 | tf_op jit(solution)/shard_map/reduce_scatter | solution.py:269
  780.6 73.1 %reduce-scatter.7.cloned.1.call-start = ((), (), s32[]{:S(2)}) async-start(), calls=%async_computation.11 | async-start | bytes 1310720 | tf_op jit(solution)/shard_map/reduce_scatter | solution.py:310
  818.7 62.6 %reduce-scatter.5.cloned.1.call-start = ((), (), s32[]{:S(2)}) async-start(), calls=%async_computation.10 | async-start | bytes 1310720 | tf_op jit(solution)/shard_map/reduce_scatter | solution.py:307
  821.1 654.5 %all-reduce.4.cloned.1.call-start = ((), (), s32[]{:S(2)}) async-start(), calls=%async_computation.18 | async-start | bytes 33554432 | tf_op jit(solution)/shard_map/psum | solution.py:322
  884.7 9.3 copy-start.11
  884.8 9.3 copy-start.24
  888.5 26.0 %all-to-all-start.2 = ((bf16[8,64,512]{2,1,0:T(8,128)(2,1)}), bf16[8,64,512]{2,1,0:T(8,128)(2,1)S(1)}, u32[]{:S(2)}, u32[]{:S(2)}) async-start(bf16[8,64,512]{2,1,0:T(8,128)(2,1)} %bitcast.431), calls=%async_computation.2 | async-start | bytes 1048576 | tf_op jit(solution)/shard_map/all_to_all | solution.py:351
  914.5 24.6 %all-to-all-start.4 = ((bf16[8,64,512]{2,1,0:T(8,128)(2,1)}), bf16[8,64,512]{2,1,0:T(8,128)(2,1)S(1)}, u32[]{:S(2)}, u32[]{:S(2)}) async-start(bf16[8,64,512]{2,1,0:T(8,128)(2,1)} %bitcast.432), calls=%async_computation.6 | async-start | bytes 1048576 | tf_op jit(solution)/shard_map/all_to_all | solution.py:352
  918.6 24.7 %copy-start.32 = (s32[256,1]{0,1:T(1,128)S(1)}, s32[256,1]{0,1:T(1,128)}, u32[]{:S(2)}) copy-start(s32[256,1]{0,1:T(1,128)} %copy-done.31) | copy-start | bytes 3076
  939.1 48.4 %all-to-all-start.5 = ((bf16[8,64,512]{2,1,0:T(8,128)(2,1)}), bf16[8,64,512]{2,1,0:T(8,128)(2,1)}, u32[]{:S(2)}, u32[]{:S(2)}) async-start(bf16[8,64,512]{2,1,0:T(8,128)(2,1)} %bitcast.430), calls=%async_computation.9 | async-start | bytes 1048576 | tf_op jit(solution)/shard_map/all_to_all | solution.py:353
  (26 other events, 59.1 us)
Sparse Core Ops, SparseCore 0:
  463.2 15.7 all-gather.8
  481.2 16.7 all-gather.10
  500.1 16.7 all-gather.12
  672.4 18.1 all-gather.14
  772.4 26.3 reduce-scatter.10
  801.4 24.8 reduce-scatter.8
  828.8 24.8 reduce-scatter.6
  856.4 24.8 reduce-scatter.4
  888.3 587.2 all-reduce.3
where the time goes:
time: 1500 us
  local copies, waits for them, and re-layouts  715 us (48%)
  waiting for transfers between devices  587 us (39%)
  matrix products  67.5 us (4%)
  other arithmetic  43 us (3%)
  blocking collectives  40.5 us (3%)
  starting transfers between devices  28.6 us (2%)
  between operations  15 us (1%)
    psum x1, waiting for transfers between devices, body(): lax.psum((self_grad, cross_grad, jnp.stack([mixer_self, mixer_cross]), ex...  485 us
    gather x7, local copies, waits for them, and re-layouts, body(): sentence = jnp.searchsorted(ends, table, side='right')  342 us
    gather x2, local copies, waits for them, and re-layouts, body(): target = starts[sentence] // (n_lanes * rows)  48.9 us
    gather x1, local copies, waits for them, and re-layouts, body(): real_flag[sentence] > 0  48.9 us
    scatter x1, local copies, waits for them, and re-layouts, body(): slot_position = jnp.zeros((n_lanes * slots,), jnp.int32).at[landing].set(...  42 us
    dynamic_slice x48, local copies, waits for them, and re-layouts, attend_forward(): lax.map(one_pair, (split_pairs(queries), split_pairs(keys_all), split_pai...  40.8 us
    psum x1, blocking collectives, body(): lax.psum((self_grad, cross_grad, jnp.stack([mixer_self, mixer_cross]), ex...  40.5 us
    scatter x1, local copies, waits for them, and re-layouts, body(): slot_sentence = jnp.full((n_lanes * slots,), -1, jnp.int32).at[landing].s...  30.6 us
  transfers between devices with their start and end apart: 15, of which 7 were waited for; matrix products, arithmetic and copies ran while one was open for 20% of the time, Pallas kernels for 0%

commit v1 on v0

v1 whole, which is shorter than its diff:
```python
import functools

import jax
import jax.numpy as jnp
from jax import lax
from jax.experimental import pallas as pl
from jax.experimental.pallas import tpu as pltpu
from jax.sharding import PartitionSpec as P

HEAD = 64
PAIR = 2 * HEAD
MESH = pl.DeviceIdType.MESH
F32 = jnp.float32
BF16 = jnp.bfloat16
EPSILON = 1e-05
SYNTH_WEIGHT = 0.4
SCORE_FILL = -1e30
LAYER_VMEM = 55 * 1024 * 1024
FINISH_VMEM = 24 * 1024 * 1024

(
    P00, P01, P02, P03, P10, P11, P12, P13, N0, N1, X1, X2,
    OUT, RET0, RET1, NORM, SHR0, EXP0, SHR1, EXP1, CROSS_Q, CROSS_KV,
    SELF_Q, SELF_KV,
) = range(24)
(
    START, PACK1, PACK2, PLACE, SLOTS, LANE0, LANE1, LANE2, LANE3, BIAS,
    OWN0, Q0, NEAR0, FAR0, DIAG0, SATT0, SATT1, LN0, CQ, OWN1,
    KV1, NEAR1, FAR1, DIAG1, CATT0, CATT1, LN1, FFN0, FFN1, LN2,
    COT, FB0, FB1, FB2, FB3, LN1B, CROSS_B0, CROSS_B1, CROSS_ROW, CROSS_SQ,
    CROSS_SK, CROSS_SV, LN0B, MIX0, SELF_B0, SELF_B1, SELF_ROW, SELF_SQ, SELF_SK, SELF_SV,
) = range(50)
PLAN = {
    LANE0: (P00,),
    LANE1: (P01,),
    BIAS: (P02, X1, P00, P03),
    Q0: (P01, P02, N0, P10, P01),
    NEAR0: (P03,),
    FAR0: (P11, P12, P03),
    SATT1: (P13,),
    OWN1: (X2, P10),
    KV1: (P12, P11, P13, N1),
    FAR1: (P11, P13),
    LN1B: (SHR0,),
    CROSS_B1: (EXP1,),
    CROSS_SQ: (SHR1, EXP0),
    LN0B: (EXP1,),
    MIX0: (RET1, CROSS_Q, CROSS_KV, SHR0),
    SELF_B1: (RET1,),
    SELF_ROW: (EXP0,),
    SELF_SQ: (CROSS_KV, CROSS_Q),
    SELF_SK: (SHR0,),
    SELF_SV: (
        SELF_Q, EXP0, SHR0, CROSS_Q, SELF_KV, EXP1, EXP0, RET0,
        SHR0, SELF_Q, CROSS_KV, CROSS_Q, SHR0, SELF_KV, EXP0, EXP1,
        SELF_Q, SHR1, CROSS_Q, EXP0, CROSS_KV, EXP1, SELF_KV, SHR0,
        SELF_Q, CROSS_Q, SHR1, NORM, SELF_KV, CROSS_KV, EXP1, SELF_Q,
        EXP0, SHR1, CROSS_Q, SELF_Q, SHR0, RET1, SELF_KV, EXP1,
        CROSS_KV, SHR1, EXP0, NORM, SELF_KV, CROSS_KV, SELF_Q, SHR1,
        CROSS_Q, SELF_KV, RET0, EXP1, CROSS_Q, SHR1, EXP0, CROSS_KV,
        SELF_Q, EXP1, SHR0, NORM, OUT, SELF_KV, SELF_Q, SHR1,
        NORM, CROSS_KV, SELF_KV, RET0, NORM, SHR1,
    ),
}
ORDERS = {
    SHR0: (0, 2, 1, 3, 4),
    EXP0: (0, 1, 2, 3, 4),
    SHR1: (0, 2, 1, 3, 4),
    EXP1: (0, 1, 3, 2, 4),
    CROSS_Q: (0, 2, 1, 3, 4),
    CROSS_KV: (0, 3, 2, 1, 4),
    SELF_Q: (0, 2, 3, 1, 4),
    SELF_KV: (0, 1, 2, 3, 4),
}


def contract(a, b, left, right):
    return lax.dot_general(a, b, (((left,), (right,)), ((), ())), preferred_element_type=F32)


def nn(a, b):
    return contract(a, b, 1, 0)


def nt(a, b):
    return contract(a, b, 1, 1)


def tn(a, b):
    return contract(a, b, 0, 0)


def block(index, size):
    if isinstance(index, int):
        return pl.ds(index * size, size)
    return pl.ds(pl.multiple_of(index * size, size), size)


def rows_at(offset, size):
    if isinstance(offset, int):
        return pl.ds(offset, size)
    return pl.ds(pl.multiple_of(offset, 16), size)


def loop(count, step):
    def body(index, carry):
        step(index)
        return carry

    lax.fori_loop(0, count, body, 0)


def iota(shape, axis):
    return lax.broadcasted_iota(jnp.int32, shape, axis)


class Sizes:
    def __init__(self, n_dp, n_seq, rows, width, ff, sentences):
        self.n_dp, self.n_seq, self.rows, self.width, self.ff = n_dp, n_seq, rows, width, ff
        self.cap = 2 * rows // n_dp
        self.group_sents = sentences // n_dp
        self.parts = max(1, 16 // self.cap)
        self.prow = self.cap * self.parts
        self.pcol = width // self.parts
        self.slots = n_dp * self.prow
        self.passes = self.parts == 1
        self.lanes_packed = n_seq if self.passes else 1
        self.keys = n_seq * rows
        self.pairs = width // PAIR
        self.ff_blocks = ff // width
        lane_bits = [("seq", b) for b in range(n_seq.bit_length() - 1)]
        dp_bits = [("dp", b) for b in range(n_dp.bit_length() - 1)]
        self.planned = (n_dp, n_seq) == (8, 4)
        links = (("seq", 0), ("dp", 0), ("seq", 1), ("dp", 1), ("dp", 2))
        self.order_a = lane_bits[:1] + dp_bits[:2] + lane_bits[1:] + dp_bits[2:]
        self.order_b = lane_bits + dp_bits[1:2] + dp_bits[:1] + dp_bits[2:]
        self.stages = len(self.order_a)
        w = width
        self.units, row = {}, 0
        half = self.ff_blocks // 2
        names = [(name, half) for name in (SHR0, EXP0, SHR1, EXP1)]
        names += [(name, 2) for name in (CROSS_Q, CROSS_KV, SELF_Q, SELF_KV)]
        for name, blocks in names:
            order = (self.order_a, self.order_b)[len(self.units) % 2]
            if self.planned:
                order = [links[c] for c in ORDERS[name]]
            self.units[name] = (len(self.units), row, blocks * w, 0, w, order)
            row += blocks * w
        self.sum_rows = row
        self.land, spot = {}, 0
        for name, (_, _, count, _, _, _) in self.units.items():
            self.land[name] = spot
            n = count
            for s in range(self.stages):
                n = n // 2 if self.halves(n, s) else n
                spot += n
        self.land_rows = spot

    def halves(self, count, stage):
        return count % 32 == 0 and stage < self.stages - 1


def scratch_list(z):
    w, r, k = z.width, z.rows, z.keys
    v = pltpu.VMEM
    dma = pltpu.SemaphoreType.DMA
    n_units = len(z.units)
    if z.passes:
        extra = {"passed": v((2, 3, z.slots, z.pcol), BF16)}
    else:
        extra = {"hidden": v((z.ff_blocks, r, w), BF16)}
    return extra | {
        "row_io": v((3, r, w), BF16),
        "w_self": v((3, w, w), BF16),
        "w_cross": v((3, w, w), BF16),
        "w_mix": v((2, w, w), BF16),
        "w_exp": v((z.ff, w), BF16),
        "w_shr": v((z.ff, w), BF16),
        "packed": v((3, z.slots, z.pcol), BF16),
        "landed": v((3, z.slots, z.pcol), BF16),
        "back": v((3, z.slots, z.pcol), BF16),
        "place": v((z.parts, z.slots, r), BF16),
        "place_t": v((z.parts, r, z.slots), BF16),
        "compact": v((z.lanes_packed, z.parts, r, z.slots), BF16),
        "row_local": v((r, 128), F32),
        "bias": v((2, k, r), F32),
        "all_rows": v((2, k, w), BF16),
        "query": v((2, r, w), BF16),
        "key": v((2, k, w), BF16),
        "value": v((2, k, w), BF16),
        "score": v((k, 2 * r), F32),
        "lifted": v((2, z.pairs, k, 2 * r), BF16),
        "mixed_t": v((2, z.pairs, PAIR, r), BF16),
        "inverse": v((2, z.pairs, 8, 2 * r), F32),
        "mixed": v((2, r, w), BF16),
        "unit": v((3, r, w), F32),
        "spread": v((3, r, 128), F32),
        "stream": v((r, w), F32),
        "stream_low": v((2, r, w), BF16),
        "grad_in": v((r, w), BF16),
        "grad_q": v((r, w), BF16),
        "held": v((2, 2 * r, w), BF16),
        "held_y": v((2, r, w), BF16),
        "arrived": v((z.land_rows, w), BF16),
        "norm_acc": v((z.stages + 1, 8, w), F32),
        "norm_in": v((z.stages, 8, w), F32),
        "arrival": v((z.n_dp * z.n_seq * r // 128, 128), jnp.int32),
        "lengths": pltpu.SMEM((z.n_dp * z.group_sents,), jnp.int32),
        "flags": pltpu.SMEM((z.n_dp * z.group_sents,), jnp.int32),
        "gains": v((3, w), F32),
        "shifts": v((3, w), F32),
        "load_sem": dma((8,)),
        "small_sem": dma((5,)),
        "in_send": dma((3,)),
        "in_recv": dma((3, 4)),
        "back_send": dma((3,)),
        "back_recv": dma((3, 4)),
        "all_send": dma((2, 3, 4)),
        "all_recv": dma((2, 3, 4)),
        "part_send": dma((2, 3)),
        "part_recv": dma((2, 3)),
        "sum_send": dma((n_units, z.stages)),
        "sum_recv": dma((n_units, z.stages)),
        "sum_free": pltpu.SemaphoreType.REGULAR((n_units, z.stages)),
        "full_send": dma(()),
        "full_recv": dma((n_units, z.stages)),
        "norm_send": dma((z.stages,)),
        "norm_recv": dma((z.stages,)),
    }


INPUTS = (
    "arrival_hbm",
    "lengths_hbm",
    "flags_hbm",
    "tokens",
    "memory",
    "cotangent",
    "self_proj",
    "cross_proj",
    "mixers",
    "expander",
    "shrinker",
    "gains_hbm",
    "shifts_hbm",
)
OUTPUTS = ("layer_out", "token_grad", "memory_grad", "sums", "g_norm")


class Refs:
    pass


def layer_kernel(z, names, *refs):
    t = Refs()
    for name, ref in zip(names, refs):
        setattr(t, name, ref)
    group = lax.axis_index("dp")
    lane = lax.axis_index("seq")
    device = group * z.n_seq + lane
    rows, width, keys = z.rows, z.width, z.keys
    wide = lambda value: jnp.concatenate([value, value], axis=1)
    def partner(axis, bit):
        index = group if axis == "dp" else lane
        step = 1 << bit
        high = lax.rem(lax.div(index, step), 2)
        other = index + step * (1 - 2 * high)
        return high, other, ((other, lane) if axis == "dp" else (group, other))

    inputs = [
        pltpu.make_async_copy(source, t.row_io.at[k], t.load_sem.at[k])
        for k, source in enumerate((t.tokens, t.memory, t.cotangent))
    ]
    weights = [
        pltpu.make_async_copy(t.self_proj, t.w_self, t.load_sem.at[3]),
        pltpu.make_async_copy(t.mixers, t.w_mix, t.load_sem.at[4]),
        pltpu.make_async_copy(t.cross_proj, t.w_cross, t.load_sem.at[5]),
        pltpu.make_async_copy(t.shrinker, t.w_shr, t.load_sem.at[6]),
    ]
    for j in range(z.ff_blocks):
        weights.append(
            pltpu.make_async_copy(
                t.expander.at[:, block(j, width)], t.w_exp.at[block(j, width)], t.load_sem.at[7]
            )
        )
    small = [
        pltpu.make_async_copy(getattr(t, name + "_hbm"), getattr(t, name), t.small_sem.at[i])
        for i, name in enumerate(("arrival", "lengths", "flags", "gains", "shifts"))
    ]
    for copy in small[:1] + inputs + small[1:]:
        copy.start()

    barrier = pltpu.get_barrier_semaphore()

    def greet(j, carry):
        to = lax.rem(group + j, z.n_dp)
        pl.semaphore_signal(barrier, inc=1, device_id=(to, lane), device_id_type=MESH)
        return carry

    lax.fori_loop(1, z.n_dp, greet, 0)
    for j in range(1, z.n_seq):
        to = lax.rem(lane + j, z.n_seq)
        pl.semaphore_signal(barrier, inc=1, device_id=(group, to), device_id_type=MESH)

    shift = (z.n_seq * rows).bit_length() - 1
    small[0].wait()
    strips = rows // 128
    mine = t.arrival[pl.ds(device * strips, strips), :]
    mine = jnp.concatenate([mine[i : i + 1] for i in range(strips)], axis=1)
    target = lax.shift_right_logical(mine, shift)
    hit = jnp.where(iota((z.n_dp, rows), 0) == target, 1.0, 0.0)
    earlier = jnp.where(iota((rows, rows), 0) < iota((rows, rows), 1), 1.0, 0.0).astype(BF16)
    rank = jnp.sum(hit * nn(hit.astype(BF16), earlier), axis=0, keepdims=True)
    place = target * z.prow + rank.astype(jnp.int32)
    for part in range(z.parts):
        picks = jnp.where(iota((z.slots, rows), 0) == place + part * z.cap, 1.0, 0.0)
        t.place[part] = picks.astype(BF16)

    def pack(k, selector, source):
        total = None
        for part in range(z.parts):
            piece = source[:, part * z.pcol : (part + 1) * z.pcol]
            term = nn(selector[part], piece)
            total = term if total is None else total + term
        t.packed[k] = total.astype(BF16)

    quarter_size = z.n_dp // 4
    quarter, member = lax.div(group, quarter_size), lax.rem(group, quarter_size)
    quarter_rows = quarter_size * z.prow

    def crossed(i):
        high = lax.rem(lax.div(quarter, 2) + i // 2, 2)
        return 2 * high + lax.rem(lax.rem(quarter, 2) + i % 2, 2)

    def send_rows(k, landing, send_sem, recv_sem):
        own = block(group, z.prow)
        done = recv_sem.at[k, quarter]
        pltpu.make_async_copy(t.packed.at[k, own], landing.at[k, own], done).start()
        for i in (3, 2, 1, 0):
            first = crossed(i) * quarter_size

            def one(j, carry):
                to = first + lax.rem(member + j, quarter_size)
                pltpu.make_async_remote_copy(
                    src_ref=t.packed.at[k, block(to, z.prow)],
                    dst_ref=landing.at[k, own],
                    send_sem=send_sem.at[k],
                    recv_sem=done,
                    device_id=(to, lane),
                    device_id_type=MESH,
                ).start()
                return carry

            lax.fori_loop(1 if i == 0 else 0, quarter_size, one, 0)

    def wait_quarter(k, landing, recv_sem, i):
        which = crossed(i)
        at = landing.at[k, block(which, quarter_rows)]
        pltpu.make_async_copy(at, at, recv_sem.at[k, which]).wait()
        return block(which, quarter_rows)

    def wait_rows(k, landing, recv_sem):
        for i in range(4):
            wait_quarter(k, landing, recv_sem, i)

    def wait_sent(k, send_sem):
        others = pl.ds(0, (z.n_dp - 1) * z.prow)
        pltpu.make_async_copy(
            t.packed.at[k, others], t.packed.at[k, others], send_sem.at[k]
        ).wait()

    inputs[0].wait()
    pack(0, t.place, t.row_io[0])
    pl.semaphore_wait(barrier, z.n_dp - 1 + z.n_seq - 1)

    running, gathered, landed_count, exchanged, given = {}, {}, {}, set(), []

    def advance(name):
        try:
            next(running[name])
        except StopIteration:
            del running[name]

    def begin(name, task):
        next(task)
        running[name] = task

    def step(piece):
        if not z.planned:
            for name in list(running):
                advance(name)
            return
        for name in PLAN.get(piece, ()):
            if name in (X1, X2):
                start_exchange(1 + name - X1)
            elif name in running:
                advance(name)

    def finish(done=lambda: False):
        while running and not done():
            for name in list(running):
                advance(name)

    def start_exchange(k):
        if k in exchanged:
            return
        exchanged.add(k)
        send_rows(k, t.landed, t.in_send, t.in_recv)
        if z.passes and k < 2:
            for i in range(4):
                begin(P00 + 4 * k + i, pass_on(k, i))

    near_lane, near = partner("seq", 0)[1:]
    far_lane, far = partner("seq", 1)[1:]
    lanes = (lane, near_lane, far_lane, near_lane + (far_lane - lane))

    def passing(k, source, at, which, sem, to):
        return pltpu.make_async_remote_copy(
            src_ref=source.at[at],
            dst_ref=t.passed.at[k, which, at],
            send_sem=t.all_send.at[k, which, sem],
            recv_sem=t.all_recv.at[k, which, sem],
            device_id=to,
            device_id_type=MESH,
        )

    def pass_on(k, i):
        yield
        at = wait_quarter(k, t.landed, t.in_recv, i)
        landed_count[k] = landed_count.get(k, 0) + 1
        to_far = passing(k, t.landed.at[k], at, 0, i, far)
        to_far.start()
        yield
        to_far.wait()
        gathered[k, 0] = gathered.get((k, 0), 0) + 1
        if i % 2 == 1:
            half_at = block(lax.div(crossed(i), 2), 2 * quarter_rows)
            relay = passing(k, t.passed.at[k, 0], half_at, 2, i // 2, near)
            relay.start()
            yield
            relay.wait()
            gathered[k, 2] = gathered.get((k, 2), 0) + 2

    def pass_near(k):
        to_near = passing(k, t.landed.at[k], pl.ds(0, z.slots), 1, 0, near)
        to_near.start()
        yield
        to_near.wait()
        gathered[k, 1] = 4

    start_exchange(0)
    for copy in weights:
        copy.start()
    step(START)
    for k in (1, 2):
        inputs[k].wait()
        pack(k, t.place, t.row_io[k])
        step(PACK1 + k - 1)

    place_down = jnp.transpose(jnp.broadcast_to(place.astype(F32), (128, rows)))[:, 0:1].astype(jnp.int32)
    for part in range(z.parts):
        picks = jnp.where(iota((rows, z.slots), 1) == place_down + part * z.cap, 1.0, 0.0)
        t.place_t[part] = picks.astype(BF16)
    step(PLACE)
    n_all = z.n_dp * z.n_seq
    arrival = [t.arrival[pl.ds(i, n_all, stride=strips), :] for i in range(strips)]
    arrival = jnp.concatenate(arrival, axis=1)
    whose = lax.shift_right_logical(arrival, shift)
    ours = jnp.where(whose == group, 1.0, 0.0)
    local = (arrival - whose * (z.n_seq * rows)).astype(F32)
    within = nn(ours.astype(BF16), earlier)
    key_local = t.score.at[:, 0:128]
    rank_at = t.bias.at[0, 0:n_all, :]
    local_at = t.bias.at[0, n_all : 2 * n_all, :]
    rank_at[...] = jnp.where(ours > 0.5, within, -1.0)
    local_at[...] = local
    digits = t.lifted.at[1, 0]

    def slot_locals(index):
        chosen = rank_at[pl.ds(index, 1), :] == iota((z.prow, rows), 0).astype(F32)
        found = jnp.where(chosen, local_at[pl.ds(index, 1), :], 0.0)
        found = jnp.sum(found, axis=1, keepdims=True)
        high = jnp.floor(found * (1.0 / 32))
        pair = jnp.where(iota((z.prow, 128), 1) == 0, high, found - 32.0 * high)
        source, other = index // z.n_seq, index % z.n_seq
        digits[block(source, z.prow), block(other, 128)] = pair.astype(BF16)

    loop(n_all, slot_locals)
    step(SLOTS)
    down, across = iota((n_all, n_all), 0), iota((n_all, n_all), 1)
    same_lane = (down & (z.n_seq - 1)) == (across & (z.n_seq - 1))
    count_row = nt(jnp.ones((16, rows), BF16), ours.astype(BF16))
    after = jnp.where(same_lane & (down < across), 1.0, 0.0).astype(BF16)
    base_row = nn(count_row.astype(BF16), after)
    first_row = jnp.where(count_row > 0.5, base_row, -1024.0).astype(BF16)
    in_block = iota((1, z.slots), 1) & (z.prow - 1)
    from_source = lax.shift_right_logical(iota((n_all, z.slots), 1), z.prow.bit_length() - 1)
    for index in range(z.n_seq):
        wanted = from_source * z.n_seq + lanes[index]
        expand = jnp.where(iota((n_all, z.slots), 0) == wanted, 1.0, 0.0).astype(BF16)
        spot_row = nn(first_row, expand)[0:1, :].astype(jnp.int32)
        for part in range(z.parts):
            offset = in_block - part * z.cap
            spot = jnp.where((offset >= 0) & (offset < z.cap), spot_row + offset, -1)
            picks = jnp.where(spot == iota((rows, z.slots), 0), 1.0, 0.0).astype(BF16)
            if index < z.lanes_packed:
                t.compact[index, part] = picks
            if part == 0:
                found = nn(picks, digits[0 : z.slots, block(lanes[index], 128)])
                found = 32.0 * found[:, 0:1] + found[:, 1:2]
                key_local[block(lanes[index], rows), :] = jnp.broadcast_to(found, (rows, 128))
            if index == 0:
                spot_tall = jnp.broadcast_to(spot.astype(F32), (128, z.slots))
                spot_down = jnp.transpose(spot_tall)[:, 0:1].astype(jnp.int32)
                picks = jnp.where(spot_down == iota((z.slots, rows), 1), 1.0, 0.0)
                t.place[part] = picks.astype(BF16)
        step(LANE0 + index)

    def sentence_of(index):
        start, end, weight = jnp.zeros_like(index), jnp.zeros_like(index), jnp.zeros_like(index)
        edge = 0
        for j in range(z.group_sents):
            sentence = group * z.group_sents + j
            after = edge + t.lengths[sentence]
            low, high = jnp.float32(edge), after.astype(F32)
            share = jnp.where(t.flags[sentence] == 1, 1.0, SYNTH_WEIGHT)
            here = index >= low
            start = jnp.where(here, low, start)
            end = jnp.where(here, high, end)
            weight = jnp.where(here, share, weight)
            edge = after
        return start, end, weight

    for copy in small[1:]:
        copy.wait()
    own_local = key_local[block(lane, rows), :]
    t.row_local[...] = sentence_of(own_local)[2]
    query_local = jnp.transpose(own_local)[0:1, :]
    query_start, query_end, _ = sentence_of(query_local)

    def make_bias(j):
        here = key_local[block(j, rows), 0:1]
        late = here >= query_start
        t.bias[0, block(j, rows), :] = jnp.where(late & (here <= query_local), 0.0, SCORE_FILL)
        t.bias[1, block(j, rows), :] = jnp.where(late & (here < query_end), 0.0, SCORE_FILL)

    loop(z.n_seq, make_bias)
    step(BIAS)

    def unpack(selector, source):
        pieces = [nn(selector[part], source) for part in range(z.parts)]
        return pieces[0] if z.parts == 1 else jnp.concatenate(pieces, axis=1)

    def gather_seq(k):
        held = t.all_rows

        def copy(what, which, to):
            return pltpu.make_async_remote_copy(
                src_ref=held.at[k, what],
                dst_ref=held.at[k, what],
                send_sem=t.all_send.at[k, which, 0],
                recv_sem=t.all_recv.at[k, which, 0],
                device_id=to,
                device_id_type=MESH,
            )

        ours = block(lane, rows)
        to_far, to_near = copy(ours, 0, far), copy(ours, 1, near)
        relay = copy(block(far_lane, rows), 2, near)
        to_far.start()
        to_near.start()
        yield
        to_near.wait()
        to_far.wait()
        relay.start()
        gathered[k, 0] = gathered[k, 1] = 4
        yield
        relay.wait()
        gathered[k, 2] = 4

    def own_rows(k):
        if z.passes:
            finish(lambda: landed_count.get(k) == 4)
            begin(N0 + k, pass_near(k))
        else:
            wait_rows(k, t.landed, t.in_recv)
        t.all_rows[k, block(lane, rows), :] = unpack(t.compact.at[0], t.landed[k]).astype(BF16)
        if not z.passes:
            begin(N0 + k, gather_seq(k))

    def other_rows(k, which):
        finish(lambda: gathered.get((k, which)) == 4)
        index = (2, 1, 3)[which]
        if z.passes:
            found = unpack(t.compact.at[index], t.passed[k, which]).astype(BF16)
            t.all_rows[k, block(lanes[index], rows), :] = found
        return lanes[index]

    lanes_low = iota((rows, PAIR), 1) < HEAD
    tall_low = iota((PAIR, rows), 0) < HEAD
    none = jnp.zeros((), BF16)

    def stacked_queries(branch, p):
        pair = t.query[branch, :, block(p, PAIR)]
        return jnp.concatenate(
            [jnp.where(lanes_low, pair, none), jnp.where(lanes_low, none, pair)], axis=0
        )

    def stacked_tall(tall):
        return jnp.concatenate(
            [jnp.where(tall_low, tall, 0.0), jnp.where(tall_low, 0.0, tall)], axis=1
        )

    def split_pair(both):
        return jnp.concatenate([both[:HEAD, :rows], both[HEAD:, rows:]], axis=0)

    def attend_pair(branch, p):
        cols = block(p, PAIR)
        tall = jnp.transpose(t.query[branch, :, cols].astype(F32))
        stacked = stacked_tall(tall).astype(BF16)

        def scores(j, peak):
            at = block(j, rows)
            score = nn(t.key[branch, at, cols], stacked) + wide(t.bias[branch, at, :])
            t.score[at, :] = score
            return jnp.maximum(peak, jnp.max(score, axis=0, keepdims=True))

        peak = jnp.full((1, 2 * rows), -3e38, F32)
        for j in range(z.n_seq):
            peak = scores(j, peak)

        def lift(j, carry):
            total, mixed = carry
            at = block(j, rows)
            lifted = jnp.exp(t.score[at, :] - peak)
            low = lifted.astype(BF16)
            t.lifted[branch, p, at, :] = low
            return (
                total + jnp.sum(lifted, axis=0, keepdims=True),
                mixed + tn(t.value[branch, at, cols], low),
            )

        sums = (jnp.zeros((1, 2 * rows), F32), jnp.zeros((PAIR, 2 * rows), F32))
        for j in range(z.n_seq):
            sums = lift(j, sums)
        total, mixed = sums
        inverse = 1.0 / total
        t.inverse[branch, p] = jnp.broadcast_to(inverse, (8, 2 * rows))
        tall = split_pair(mixed * inverse)
        t.mixed_t[branch, p] = tall.astype(BF16)
        t.mixed[branch, :, cols] = jnp.transpose(tall).astype(BF16)

    def attend_back_pair(branch, p):
        cols = block(p, PAIR)
        stacked = stacked_queries(branch, p)
        inverse = t.inverse[branch, p, 0:1, :]
        tall = jnp.transpose(t.grad_in[:, cols].astype(F32))
        product = tall * t.mixed_t[branch, p].astype(F32)
        inner = inverse * jnp.concatenate(
            [
                jnp.sum(product[:HEAD], axis=0, keepdims=True),
                jnp.sum(product[HEAD:], axis=0, keepdims=True),
            ],
            axis=1,
        )
        both = stacked_tall(tall) * inverse
        both_down = jnp.transpose(both).astype(BF16)
        both = both.astype(BF16)

        def one(j, query_grad):
            at = block(j, rows)
            low = t.lifted[branch, p, at, :]
            prob_grad = nn(t.value[branch, at, cols], both)
            score_grad = (low.astype(F32) * (prob_grad - inner)).astype(BF16)
            t.w_shr[at, cols] = nn(score_grad, stacked).astype(BF16)
            t.w_shr[rows_at(keys + j * rows, rows), cols] = nn(low, both_down).astype(BF16)
            return query_grad + tn(t.key[branch, at, cols], score_grad)

        query_grad = jnp.zeros((PAIR, 2 * rows), F32)
        for j in range(z.n_seq):
            query_grad = one(j, query_grad)
        tall_grad = split_pair(query_grad) * HEAD ** (-0.5)
        t.grad_q[:, cols] = jnp.transpose(tall_grad).astype(BF16)

    def project_keys(branch, weight, j):
        at = block(j, rows)
        source = t.all_rows[branch, at, :]
        t.key[branch, at, :] = nn(source, weight[1]).astype(BF16)
        t.value[branch, at, :] = nn(source, weight[2]).astype(BF16)

    def norm_forward(values, i):
        center = values - jnp.sum(values, axis=-1, keepdims=True) * (1.0 / width)
        var = jnp.sum(center * center, axis=-1, keepdims=True) * (1.0 / width)
        scale = lax.rsqrt(var + EPSILON)
        unit = center * scale
        t.unit[i] = unit
        t.spread[i] = jnp.broadcast_to(scale, (rows, 128))
        return unit * t.gains[i : i + 1, :] + t.shifts[i : i + 1, :]

    def norm_backward(grad, i):
        unit = t.unit[i]
        t.norm_acc[0, i : i + 1, :] = jnp.sum(grad * unit, axis=0, keepdims=True)
        t.norm_acc[0, 3 + i : 4 + i, :] = jnp.sum(grad, axis=0, keepdims=True)
        scaled = grad * t.gains[i : i + 1, :]
        mean = jnp.sum(scaled, axis=-1, keepdims=True) * (1.0 / width)
        slope = jnp.sum(scaled * unit, axis=-1, keepdims=True) * (1.0 / width)
        return (scaled - mean - unit * slope) * t.spread[i, :, 0:1]

    def add_rows(offset, spot, count, cols):
        tile = next(s for s in (128, 96, 64, 48, 32, 16) if count % s == 0)

        def one(i):
            at = rows_at(offset + i * tile, tile)
            t.sums[at, cols] += t.arrived[rows_at(spot + i * tile, tile), cols]

        loop(count // tile, one)

    def sum_unit(name):
        unit, offset, count, first_col, n_cols, order = z.units[name]
        cols = pl.ds(first_col, n_cols)
        spot = z.land[name]
        halved = []
        for s, (axis, bit) in enumerate(order):
            high, _, to = partner(axis, bit)
            halving = z.halves(count, s)
            if halving:
                count //= 2
                keep, give = offset + high * count, offset + (1 - high) * count
                halved.append((s, high, to, axis, bit))
            else:
                keep = give = offset
            copy = pltpu.make_async_remote_copy(
                src_ref=t.sums.at[rows_at(give, count), cols],
                dst_ref=t.arrived.at[rows_at(spot, count), cols],
                send_sem=t.sum_send.at[unit, s],
                recv_sem=t.sum_recv.at[unit, s],
                device_id=to,
                device_id_type=MESH,
            )
            copy.start()
            yield
            copy.wait()
            if halving:
                pl.semaphore_signal(
                    t.sum_free.at[unit, s], inc=1, device_id=to, device_id_type=MESH
                )
            add_rows(keep, spot, count, cols)
            offset = keep
            spot += count
        for s, high, to, axis, bit in reversed(halved):
            held = t.sums.at[rows_at(offset, count), cols]
            copy = pltpu.make_async_remote_copy(
                src_ref=held,
                dst_ref=held,
                send_sem=t.full_send,
                recv_sem=t.full_recv.at[unit, s],
                device_id=to,
                device_id_type=MESH,
            )
            pl.semaphore_wait(t.sum_free.at[unit, s], 1)
            copy.start()
            given.append(count)
            yield
            copy.wait_recv()
            offset = offset - high * count
            count *= 2

    def sum_norms():
        for s, (axis, bit) in enumerate(z.order_a):
            _, _, to = partner(axis, bit)
            copy = pltpu.make_async_remote_copy(
                src_ref=t.norm_acc.at[s],
                dst_ref=t.norm_in.at[s],
                send_sem=t.norm_send.at[s],
                recv_sem=t.norm_recv.at[s],
                device_id=to,
                device_id_type=MESH,
            )
            copy.start()
            yield
            copy.wait()
            t.norm_acc[s + 1] = t.norm_acc[s] + t.norm_in[s]
        t.g_norm[...] = t.norm_acc[z.stages]

    def return_rows(k):
        wait_sent(k, t.in_send)
        pack(k, t.place, t.row_io[k])
        send_rows(k, t.back, t.back_send, t.back_recv)

    def return_part(branch, k, result):
        first = branch * keys
        cross_lane = lanes[3]

        def at(which):
            return rows_at(first + which * rows, rows)

        def copy(source, landing, which, to):
            return pltpu.make_async_remote_copy(
                src_ref=source,
                dst_ref=landing,
                send_sem=t.part_send.at[branch, which],
                recv_sem=t.part_recv.at[branch, which],
                device_id=to,
                device_id_type=MESH,
            )

        one = copy(t.w_exp.at[at(cross_lane)], t.held.at[branch, pl.ds(rows, rows)], 0, near)
        two = copy(t.w_exp.at[at(near_lane)], t.held.at[branch, pl.ds(0, rows)], 1, near)
        one.start()
        two.start()
        yield
        one.wait()
        t.w_exp[at(far_lane), :] = (
            t.w_exp[at(far_lane), :].astype(F32) + t.held[branch, rows:, :].astype(F32)
        ).astype(BF16)
        three = copy(t.w_exp.at[at(far_lane)], t.held_y.at[branch], 2, far)
        three.start()
        two.wait()
        yield
        three.wait()
        total = (
            t.w_exp[at(lane), :].astype(F32)
            + t.held[branch, :rows, :].astype(F32)
            + t.held_y[branch].astype(F32)
        )
        t.row_io[k] = total.astype(BF16)
        yield from bring_back(k, result)

    def bring_back(k, result):
        return_rows(k)
        yield
        wait_rows(k, t.back, t.back_recv)
        wait_sent(k, t.back_send)
        result[...] = unpack(t.place_t, t.back[k]).astype(BF16)

    def put_sum(name, j, value):
        first = z.units[name][1] + j * width
        t.sums[pl.ds(first, width), :] = value.astype(BF16)

    own = block(lane, rows)
    own_rows(0)
    start_exchange(1)
    step(OWN0)
    weights[0].wait()
    tokens = t.all_rows[0, own, :]
    t.query[0] = (nn(tokens, t.w_self[0]).astype(BF16).astype(F32) * HEAD ** (-0.5)).astype(BF16)
    project_keys(0, t.w_self, lane)
    step(Q0)
    for which, piece in ((1, NEAR0), (0, FAR0), (2, DIAG0)):
        project_keys(0, t.w_self, other_rows(0, which))
        step(piece)
    half = z.pairs // 2
    loop(half, functools.partial(attend_pair, 0))
    step(SATT0)
    loop(z.pairs - half, lambda p: attend_pair(0, half + p))
    step(SATT1)
    weights[1].wait()
    weights[2].wait()
    first = norm_forward(t.all_rows[0, own, :].astype(F32) + nn(t.mixed[0], t.w_mix[0]), 0)
    t.stream[...] = first
    t.stream_low[0] = first.astype(BF16)
    step(LN0)
    cross_query = nn(t.stream_low[0], t.w_cross[0]).astype(BF16)
    t.query[1] = (cross_query.astype(F32) * HEAD ** (-0.5)).astype(BF16)
    step(CQ)
    own_rows(1)
    start_exchange(2)
    step(OWN1)
    project_keys(1, t.w_cross, lane)
    step(KV1)
    for which, piece in ((1, NEAR1), (0, FAR1), (2, DIAG1)):
        project_keys(1, t.w_cross, other_rows(1, which))
        step(piece)
    loop(half, functools.partial(attend_pair, 1))
    step(CATT0)
    loop(z.pairs - half, lambda p: attend_pair(1, half + p))
    step(CATT1)

    second = norm_forward(t.stream[...] + nn(t.mixed[1], t.w_mix[1]), 1)
    t.stream[...] = second
    t.stream_low[1] = second.astype(BF16)
    for copy in weights[3:]:
        copy.wait()
    step(LN1)

    def hidden_at(j):
        if z.passes:
            return t.passed.at[0, j // 2, block(j % 2, rows), :]
        return t.hidden.at[j]

    def expand_block(j):
        pre = nn(t.stream_low[1], t.w_exp[block(j, width), :])
        gate = 0.5 + 0.5 * jnp.tanh(0.5 * pre)
        hidden = (pre * gate).astype(BF16)
        hidden_at(j)[...] = hidden
        t.score[block(j, rows), :] = gate * (1.0 + pre * (1.0 - gate))
        t.stream[...] += nn(hidden, t.w_shr[block(j, width), :])

    half = z.ff_blocks // 2
    for part in range(2):
        for j in range(half):
            expand_block(part * half + j)
        step(FFN0 + part)
    t.row_io[0] = norm_forward(t.stream[...], 2).astype(BF16)
    begin(OUT, bring_back(0, t.layer_out))
    step(LN2)

    wait_rows(2, t.landed, t.in_recv)
    grad = unpack(t.compact.at[0], t.landed[2]) * t.row_local[:, 0:1]
    t.stream[...] = norm_backward(grad, 2)
    t.grad_in[...] = t.stream[...].astype(BF16)
    step(COT)

    half = z.ff_blocks // 2
    for part, name in enumerate((SHR0, SHR1)):
        for j in range(half):
            put_sum(name, j, tn(hidden_at(part * half + j)[...], t.grad_in[...]))
        begin(name, sum_unit(name))
        step(FB0 + part)

    def expand_back(part, j, name):
        cols = block(part * half + j, width)
        pre_grad = nt(t.grad_in[...], t.w_shr[cols, :]) * t.score[block(part * half + j, rows), :]
        low = pre_grad.astype(BF16)
        put_sum(name, j, tn(t.stream_low[1], low))
        t.stream[...] += nt(low, t.w_exp[cols, :])

    for part, name in enumerate((EXP0, EXP1)):
        for j in range(half):
            expand_back(part, j, name)
        begin(name, sum_unit(name))
        step(FB2 + part)
    t.stream[...] = norm_backward(t.stream[...], 1)
    low = t.stream[...].astype(BF16)
    put_sum(CROSS_Q, 0, tn(t.mixed[1], low))
    t.grad_in[...] = nt(low, t.w_mix[1]).astype(BF16)
    step(LN1B)

    def row_part(branch, weight):
        def one(j):
            at = block(j, rows)
            total = nt(t.w_shr[at, :], weight[1]) + nt(
                t.w_shr[rows_at(keys + j * rows, rows), :], weight[2]
            )
            t.w_exp[rows_at(branch * keys + j * rows, rows), :] = total.astype(BF16)

        loop(z.n_seq, one)

    def key_sums(branch, which):
        first = which * keys

        def one(j, total):
            return total + tn(
                t.all_rows[branch, block(j, rows), :], t.w_shr[rows_at(first + j * rows, rows), :]
            )

        return lax.fori_loop(0, z.n_seq, one, jnp.zeros((width, width), F32))

    def attention_back(branch, weight, first, source, k, result):
        q_sum, kv_sum = ((SELF_Q, SELF_KV), (CROSS_Q, CROSS_KV))[branch]
        half = z.pairs // 2
        for part in range(2):
            loop(half, lambda p: attend_back_pair(branch, part * half + p))
            step(first + part)
        row_part(branch, weight)
        if branch == 0:
            t.w_exp[own, :] = (
                t.w_exp[own, :].astype(F32) + t.stream[...] + nt(t.grad_q[...], weight[0])
            ).astype(BF16)
        begin(RET0 + branch, return_part(branch, k, result))
        step(first + 2)
        put_sum(q_sum, 1, tn(source[...], t.grad_q[...]))
        begin(q_sum, sum_unit(q_sum))
        step(first + 3)
        put_sum(kv_sum, 0, key_sums(branch, 0))
        step(first + 4)
        put_sum(kv_sum, 1, key_sums(branch, 1))
        begin(kv_sum, sum_unit(kv_sum))
        step(first + 5)

    attention_back(1, t.w_cross, CROSS_B0, t.stream_low.at[0], 2, t.memory_grad)
    t.stream[...] = norm_backward(t.stream[...] + nt(t.grad_q[...], t.w_cross[0]), 0)
    t.norm_acc[0, 6:8, :] = jnp.zeros((2, width), F32)
    begin(NORM, sum_norms())
    step(LN0B)
    low = t.stream[...].astype(BF16)
    put_sum(SELF_Q, 0, tn(t.mixed[0], low))
    t.grad_in[...] = nt(low, t.w_mix[0]).astype(BF16)
    step(MIX0)
    attention_back(0, t.w_self, SELF_B0, t.all_rows.at[0, own], 1, t.token_grad)
    finish()
    total = t.sums.at[pl.ds(0, sum(given)), :]
    pltpu.make_async_copy(total, total, t.full_send).wait()


def finish_kernel(z, *refs):
    w = z.width
    sums, rows, norms = refs[0], refs[1:4], refs[4]
    g_self, g_cross, g_mix, g_exp, g_shr = refs[5:10]
    done, gains, shifts, full, out_sem, row_sem = refs[10:13], *refs[13:]
    copies = [pltpu.make_async_copy(a, b, row_sem.at[i]) for i, (a, b) in enumerate(zip(rows, done))]
    for copy in copies:
        copy.start()
    gains[...] = norms[0:3, :]
    shifts[...] = norms[3:6, :]
    pieces = []
    half = z.ff_blocks // 2
    for j in range(z.ff_blocks):
        for name, result in (((SHR0, SHR1)[j // half], g_shr), ((EXP0, EXP1)[j // half], g_exp)):
            spot = (block(j, w), slice(None)) if result is g_shr else (slice(None), block(j, w))
            pieces.append((z.units[name][1] + (j % half) * w, result.at[spot]))
    for j, (name, result) in enumerate(((SELF_Q, g_self), (CROSS_Q, g_cross))):
        first = z.units[name][1]
        pieces.append((first, g_mix.at[j]))
        pieces += [(first + (1 + i) * w, result.at[i]) for i in range(3)]

    def widen(first, i):
        def one(c):
            at = rows_at(first + c * 64, 64)
            full[i, block(c, 64), :] = sums[at, :].astype(F32)

        loop(w // 64, one)

    for i, (first, result) in enumerate(pieces):
        widen(first, i)
        copy = pltpu.make_async_copy(full.at[i], result, out_sem.at[i])
        copy.start()
        copies.append(copy)
    for copy in copies:
        copy.wait()


def body(
    z,
    tokens,
    memory,
    cotangent,
    arrival_order,
    lengths,
    real_flag,
    self_proj,
    cross_proj,
    mixers,
    expander,
    shrinker,
    norm_gains,
    norm_shifts,
):
    scratch = scratch_list(z)
    names = INPUTS + OUTPUTS + tuple(scratch)
    w = z.width
    anywhere = pl.BlockSpec(memory_space=pl.ANY)
    vmem = pl.BlockSpec(memory_space=pltpu.VMEM)
    results = pl.pallas_call(
        functools.partial(layer_kernel, z, names),
        out_shape=(pltpu.VMEM((z.rows, w), BF16),) * 3
        + (pltpu.VMEM((z.sum_rows, w), BF16), pltpu.VMEM((8, w), F32)),
        in_specs=[anywhere] * 13,
        out_specs=[vmem] * 5,
        scratch_shapes=list(scratch.values()),
        compiler_params=pltpu.CompilerParams(
            collective_id=0, has_side_effects=True, vmem_limit_bytes=LAYER_VMEM
        ),
        name="layer",
    )(
        arrival_order.reshape(-1, 128),
        lengths,
        real_flag,
        tokens,
        memory,
        cotangent,
        self_proj,
        cross_proj,
        mixers,
        expander,
        shrinker,
        norm_gains,
        norm_shifts,
    )
    *row_results, sums, norms = results
    n_blocks = z.sum_rows // w
    wide = [(3, w, w), (3, w, w), (2, w, w), (w, z.ff), (z.ff, w)]
    done = pl.pallas_call(
        functools.partial(finish_kernel, z),
        out_shape=tuple(jax.ShapeDtypeStruct(shape, F32) for shape in wide)
        + (jax.ShapeDtypeStruct((z.rows, w), BF16),) * 3
        + (jax.ShapeDtypeStruct((3, w), F32),) * 2,
        in_specs=[vmem] * 5,
        out_specs=[anywhere] * 8 + [vmem] * 2,
        scratch_shapes=[
            pltpu.VMEM((n_blocks, w, w), F32),
            pltpu.SemaphoreType.DMA((n_blocks,)),
            pltpu.SemaphoreType.DMA((3,)),
        ],
        compiler_params=pltpu.CompilerParams(vmem_limit_bytes=FINISH_VMEM),
        name="widen",
    )(sums, *row_results, norms)
    return (*done[5:8], *done[:5], *done[8:])


def solution(mesh):
    n_dp, n_seq = mesh.shape["dp"], mesh.shape["seq"]

    def whole(*arrays):
        tokens, lengths, expander = arrays[0], arrays[4], arrays[9]
        z = Sizes(
            n_dp,
            n_seq,
            tokens.shape[0] // (n_dp * n_seq),
            tokens.shape[1],
            expander.shape[1],
            lengths.shape[0],
        )
        split = P(("dp", "seq"), None)
        return jax.shard_map(
            functools.partial(body, z),
            mesh=mesh,
            in_specs=(split,) * 3 + (P(),) * 10,
            out_specs=(split,) * 3 + (P(),) * 7,
            check_vma=False,
        )(*arrays)

    return whole
```

time: 1500 us -> 150 us (0.10)
  local copies, waits for them, and re-layouts: 715 us -> 0 us
  waiting for transfers between devices: 587 us -> 0 us
  Pallas kernels: 0 us -> 149 us
  matrix products: 67.5 us -> 0 us
  other arithmetic: 43 us -> 0 us
  blocking collectives: 40.5 us -> 0 us
  starting transfers between devices: 28.6 us -> 0 us
    gather x25 -> x0, local copies, waits for them, and re-layouts: 486 us -> none  [the longest x7 342 us: body(): sentence = jnp.searchsorted(ends, table, side='right')]
    psum x1 -> x0, waiting for transfers between devices: 485 us -> none  [body(): lax.psum((self_grad, cross_grad, jnp.stack([mixer_self, mixer_cross]), ex...]
    pallas_call x0 -> x2, Pallas kernels: none -> 149 us  [the longest x1 143 us: body(): pl.pallas_call(functools.partial(layer_kernel, z, names), out_shape=(pltp...]
    scatter x8 -> x0, local copies, waits for them, and re-layouts: 113 us -> none  [the longest x1 42 us: body(): slot_position = jnp.zeros((n_lanes * slots,), jnp.int32).at[landing].set(...]
    dot_general x77 -> x0, matrix products: 67.5 us -> none  [the longest x16 13.3 us: pair_scores(): jnp.einsum('qhd,khd->hqk', as_heads(query_pair), as_heads(key_pair), pref...]
    all_to_all x6 -> x0, waiting for transfers between devices: 58.3 us -> none  [the longest x1 16.2 us: body(): lax.all_to_all(spread_out(token_in_grad), 'dp', split_axis=0, concat_axis...]
    reduce_scatter x4 -> x0, waiting for transfers between devices: 43.1 us -> none  [the longest x1 27.6 us: body(): lax.psum_scatter(key_part.astype(jnp.bfloat16), 'seq', scatter_dimension=...]
    dynamic_slice x50 -> x0, local copies, waits for them, and re-layouts: 40.8 us -> none  [the longest x48 40.8 us: attend_forward(): lax.map(one_pair, (split_pairs(queries), split_pairs(keys_all), split_pai...]
  transfers between devices with their start and end apart: 15 -> 0, of which waited for: 7 -> 0; matrix products, arithmetic and copies ran while one was open for 20% -> 0% of each run, Pallas kernels for 0% -> 0%
where the time goes in v1:
time: 150 us
  Pallas kernels  149 us (99%)
    pallas_call x1, Pallas kernels, body(): pl.pallas_call(functools.partial(layer_kernel, z, names), out_shape=(pltp...  143 us
    pallas_call x1, Pallas kernels, body(): pl.pallas_call(functools.partial(finish_kernel, z), out_shape=tuple((jax....  6.85 us

profile of v1, /device:TPU:0, one launch (start us, length us, event | category | flops | bytes accessed | tf_op | source)
XLA Modules:
  0.0 150.3 jit_solution(18064305065651901540)
XLA Ops:
  0.6 142.6 %layer.1 = (bf16[256,512]{1,0:T(8,128)(2,1)S(1)}, bf16[256,512]{1,0:T(8,128)(2,1)S(1)}, bf16[256,512]{1,0:T(8,128)(2,1)S(1)}, bf16[8192,512]{1,0:T(8,128)(2,1)S(1)}, f32[8,512]{1,0:T(8,128)S(1)}) custom-call(s32[64,128]{1,0:T(8,128)} %bitcast.1, s32[64]{0:T(128)} %refs_1_.1, s32[64]{0:T(128)} %refs_2_.1, bf16[256,512]{1,0:T(8,128)(2,1)} %refs_3_.1, ...), custom_call_target="tpu_custom_call" | custom-call | tf_op jit(solution)/shard_map/layer/pallas_call | solution.py:1054
  143.3 6.8 %widen.1 = (f32[3,512,512]{2,1,0:T(8,128)}, f32[3,512,512]{2,1,0:T(8,128)}, f32[2,512,512]{2,1,0:T(8,128)}, f32[512,2048]{1,0:T(8,128)}, f32[2048,512]{1,0:T(8,1...) custom-call(bf16[8192,512]{1,0:T(8,128)(2,1)S(1)} %get-tuple-element, ...), custom_call_target="tpu_custom_call" | custom-call | tf_op jit(solution)/shard_map/widen/pallas_call | solution.py:1083

commit v2 on v1

--- a/solution.py
+++ b/solution.py
@@ -719,16 +719,19 @@
         unit, offset, count, first_col, n_cols, order = z.units[name]
         cols = pl.ds(first_col, n_cols)
         spot = z.land[name]
-        halved = []
+        halved, waiting = [], None
         for s, (axis, bit) in enumerate(order):
             high, _, to = partner(axis, bit)
             halving = z.halves(count, s)
+            start = offset
             if halving:
                 count //= 2
                 keep, give = offset + high * count, offset + (1 - high) * count
                 halved.append((s, high, to, axis, bit))
             else:
                 keep = give = offset
+            if waiting is not None:
+                add_rows(give, waiting + (give - start), count, cols)
             copy = pltpu.make_async_remote_copy(
                 src_ref=t.sums.at[rows_at(give, count), cols],
                 dst_ref=t.arrived.at[rows_at(spot, count), cols],
@@ -738,15 +741,18 @@
                 device_id_type=MESH,
             )
             copy.start()
+            if waiting is not None and halving:
+                add_rows(keep, waiting + (keep - start), count, cols)
             yield
             copy.wait()
             if halving:
                 pl.semaphore_signal(
                     t.sum_free.at[unit, s], inc=1, device_id=to, device_id_type=MESH
                 )
-            add_rows(keep, spot, count, cols)
             offset = keep
+            waiting = spot
             spot += count
+        add_rows(offset, waiting, count, cols)
         for s, high, to, axis, bit in reversed(halved):
             held = t.sums.at[rows_at(offset, count), cols]
             copy = pltpu.make_async_remote_copy(

time: 150 us -> 150 us (level)
  no operation moved by 1% of the time
where the time goes in v2:
time: 150 us
  Pallas kernels  149 us (99%)
    pallas_call x1, Pallas kernels, body(): pl.pallas_call(functools.partial(layer_kernel, z, names), out_shape=(pltp...  143 us
    pallas_call x1, Pallas kernels, body(): pl.pallas_call(functools.partial(finish_kernel, z), out_shape=tuple((jax....  6.85 us

profile of v2, /device:TPU:0, one launch (start us, length us, event | category | flops | bytes accessed | tf_op | source)
XLA Modules:
  0.0 150.2 jit_solution(5967019258321433534)
XLA Ops:
  0.6 142.6 %layer.1 = (bf16[256,512]{1,0:T(8,128)(2,1)S(1)}, bf16[256,512]{1,0:T(8,128)(2,1)S(1)}, bf16[256,512]{1,0:T(8,128)(2,1)S(1)}, bf16[8192,512]{1,0:T(8,128)(2,1)S(1)}, f32[8,512]{1,0:T(8,128)S(1)}) custom-call(s32[64,128]{1,0:T(8,128)} %bitcast.1, s32[64]{0:T(128)} %refs_1_.1, s32[64]{0:T(128)} %refs_2_.1, bf16[256,512]{1,0:T(8,128)(2,1)} %refs_3_.1, ...), custom_call_target="tpu_custom_call" | custom-call | tf_op jit(solution)/shard_map/layer/pallas_call | solution.py:1060
  143.2 6.8 %widen.1 = (f32[3,512,512]{2,1,0:T(8,128)}, f32[3,512,512]{2,1,0:T(8,128)}, f32[2,512,512]{2,1,0:T(8,128)}, f32[512,2048]{1,0:T(8,128)}, f32[2048,512]{1,0:T(8,1...) custom-call(bf16[8192,512]{1,0:T(8,128)(2,1)S(1)} %get-tuple-element, ...), custom_call_target="tpu_custom_call" | custom-call | tf_op jit(solution)/shard_map/widen/pallas_call | solution.py:1089
